TPU v7x, 128 devices: a whole 4x4x4 slice. The times are simulated.
128 devices in a mesh: box: 128 (over z, x, y, core).
Axes of the slice: x: 4, y: 4, z: 4, core: 2. Of those that a mesh axis runs over, the one named last changes fastest.
Arguments:
- self_block: bfloat16 [256, 128, 512], P('box'), may hold values from -6 to 6
- interp: bfloat16 [256, 384, 128], P('box'), may hold values from -0.5 to 0.5
- split: int32 [256, 512], P('box'), may hold values from 0 to 511, each once within a row
- inverse_block: bfloat16 [256, 384, 384], P('box'), may hold values from -0.015625 to 0.015625
- row_blocks: bfloat16 [256, 8, 128, 512], P('box'), may hold values from -6 to 6
- col_blocks: bfloat16 [256, 8, 128, 512], P('box'), may hold values from -6 to 6
- pairs: int32 [256, 24, 2], P('box'), may hold values from 0 to 7
- targets: int32 [256, 24, 2], P('box'), may hold values from 0 to 6143, as said below
- pair_blocks: bfloat16 [6144, 128, 128], P('box'), may hold values from -6 to 6
Outputs:
- updated_pairs: float32 [6144, 128, 128], P('box')
- coarse_rows: float32 [128, 4, 4, 128, 128], P('box')
Inputs may be any that keep to these rules, and one draw needn't show every extreme that they name: targets[b, p, q] // 48 is an owner at most 2 devices away, along Morton order with wrap, from the device holding box b (box b lies on device b // 2); among the 96 entries of one device at most 32 name any one owner, and exactly 32 name one owner. `split`: each row is a permutation.
All inputs are finite; a program needn't handle non-finite values.
Results may differ from a plain program's by a relative error of at most 0.0047.
Values sent between devices are 32-bit elements; how exact they have to be, the bound alone decides.
No kernel may reach another device: no remote copies, remote signals or barrier semaphores. Data moves between devices by JAX's collectives and lax.ppermute only.
A program may use at most 128 MiB of HBM per device.

v0:
```python
import functools

import jax
import jax.numpy as jnp
from jax import lax
from jax.experimental import pallas as pl
from jax.experimental.pallas import tpu as pltpu
from jax.sharding import PartitionSpec as P

P_SIZE = 512
SK = 128
RD = 384
BOXES = 2
NB = 8
PAIRS = 24
SLOTS = 48
CAP = 32
ROWS = NB * SK
TILE = 256
FIRST = 32
VMEM_BYTES = 48 * 1024 * 1024
F32 = jnp.float32
BF16 = jnp.bfloat16
NT = (((1,), (1,)), ((), ()))

ANY = pl.BlockSpec(memory_space=pl.ANY)
SMEM = pl.BlockSpec(memory_space=pltpu.SMEM)
VMEM = pl.BlockSpec(memory_space=pltpu.VMEM)


def block_type(count):
    return jax.ShapeDtypeStruct((count, SK, SK), F32)


def ids_type(count):
    return jax.ShapeDtypeStruct((count,), jnp.int32)


def relation(targets, box, pair, side):
    device = lax.axis_index("box")
    devices = lax.axis_size("box")
    target = targets[box, side, pair]
    owner = lax.div(target, SLOTS)
    slot = target - owner * SLOTS
    away = owner - device
    away = jnp.where(away > devices // 2, away - devices, away)
    away = jnp.where(away < -(devices // 2), away + devices, away)
    away = jnp.where(lax.rem(device, 2) == 1, away, -away)
    return away, slot


def input_copies(hbm, vmem, sems):
    out = []
    for box in range(BOXES):
        out.append([
            pltpu.make_async_copy(source.at[box], target.at[box], sems.at[box, n])
            for n, (source, target) in enumerate(zip(hbm, vmem))
        ])
    return out


def compressor_of(split, interp, box):
    points = lax.broadcasted_iota(jnp.int32, (P_SIZE, RD), 0)
    pick_red = points == split[box:box + 1, :RD]
    points = lax.broadcasted_iota(jnp.int32, (P_SIZE, SK), 0)
    pick_skel = (points == split[box:box + 1, RD:]).astype(F32).astype(BF16)
    spread = lax.dot_general(pick_skel, interp[box], NT, preferred_element_type=F32)
    return (jnp.where(pick_red, 1.0, 0.0) - spread).astype(BF16), pick_skel


def mul(a, b):
    return jnp.dot(a, b, preferred_element_type=F32)


def products(box, copies, split, interp, inverse, rows, cols, w_far, compressor, grams):
    copies[0].wait()
    comp, pick_skel = compressor_of(split, interp, box)
    compressor[...] = comp
    copies[1].wait()

    def far(n, _):
        at = pl.ds(pl.multiple_of(n * TILE, TILE), TILE)
        w_far[at, :] = mul(cols[box, at, :], compressor[...]).astype(BF16)
        return 0

    lax.fori_loop(0, ROWS // TILE, far, 0)
    copies[2].wait()
    copies[3].wait()

    def near(n, _):
        at = pl.ds(pl.multiple_of(n * TILE, TILE), TILE)
        x_near = mul(rows[box, at, :], compressor[...]).astype(BF16)
        y_near = mul(x_near, inverse[box]).astype(BF16)
        tile = lax.dot_general(y_near, w_far[...], NT, preferred_element_type=F32)
        for k in range(TILE // SK):
            for j in range(NB):
                grams[n * (TILE // SK) + k, j] = tile[k * SK:(k + 1) * SK, j * SK:(j + 1) * SK]
        return 0

    lax.fori_loop(0, ROWS // TILE, near, 0)
    return pick_skel


def front_kernel(targets, pairs, split, interp_h, cols_h, rows_h, inverse_h, near_out, near_ids, far_out, far_ids,
                 interp, cols, rows, inverse, w_far, compressor, grams, acc, used, in_sems, out_sems):
    copies = input_copies((interp_h, cols_h, rows_h, inverse_h), (interp, cols, rows, inverse), in_sems)
    for box in range(BOXES):
        for copy in copies[box]:
            copy.start()

    def clear(n, _):
        acc[n] = jnp.zeros((SK, SK), F32)
        used[n] = 0
        return 0

    lax.fori_loop(0, 2 * SLOTS, clear, 0)

    def clear_ids(n, _):
        near_ids[n] = -1
        far_ids[n] = -1
        return 0

    lax.fori_loop(0, CAP, clear_ids, 0)

    for box in range(BOXES):
        products(box, copies[box], split, interp, inverse, rows, cols, w_far, compressor, grams)

        def add(n, _):
            pair = lax.div(n, 2)
            side = lax.rem(n, 2)
            away, slot = relation(targets, box, pair, side)

            @pl.when((away == 2) | (away == -2))
            def _():
                place = jnp.where(away == 2, slot, slot + SLOTS)
                used[place] = 1
                acc[place] = acc[place] - grams[pairs[box, side, pair], pairs[box, 1 - side, pair]]

            return 0

        lax.fori_loop(0, 2 * PAIRS, add, 0)

    for base, out, ids in ((0, near_out, near_ids), (SLOTS, far_out, far_ids)):

        def send(n, count):
            @pl.when(used[base + n] == 1)
            def _():
                ids[count] = n
                pltpu.make_async_copy(acc.at[base + n], out.at[count], out_sems.at[base + n]).start()

            return count + used[base + n]

        lax.fori_loop(0, SLOTS, send, 0)

    for base, out in ((0, near_out), (SLOTS, far_out)):

        def drain(n, _):
            @pl.when(used[base + n] == 1)
            def _():
                pltpu.make_async_copy(acc.at[base + n], out.at[0], out_sems.at[base + n]).wait()

            return 0

        lax.fori_loop(0, SLOTS, drain, 0)


def box_scratch():
    return [
        pltpu.VMEM((BOXES, RD, SK), BF16),
        pltpu.VMEM((BOXES, ROWS, P_SIZE), BF16),
        pltpu.VMEM((BOXES, ROWS, P_SIZE), BF16),
        pltpu.VMEM((BOXES, RD, RD), BF16),
        pltpu.VMEM((ROWS, RD), BF16),
        pltpu.VMEM((P_SIZE, RD), BF16),
        pltpu.VMEM((NB, NB, SK, SK), F32),
    ]


def front(targets, pairs, split, interp, cols, rows, inverse):
    return pl.pallas_call(
        front_kernel,
        out_shape=(block_type(CAP), ids_type(CAP), block_type(CAP), ids_type(CAP)),
        in_specs=[SMEM, SMEM, VMEM, ANY, ANY, ANY, ANY],
        out_specs=(ANY, SMEM, ANY, SMEM),
        scratch_shapes=box_scratch() + [
            pltpu.VMEM((2 * SLOTS, SK, SK), F32),
            pltpu.SMEM((2 * SLOTS,), jnp.int32),
            pltpu.SemaphoreType.DMA((BOXES, 4)),
            pltpu.SemaphoreType.DMA((2 * SLOTS,)),
        ],
        compiler_params=pltpu.CompilerParams(vmem_limit_bytes=VMEM_BYTES),
        cost_estimate=pl.CostEstimate(flops=4_000_000_000, bytes_accessed=10_000_000, transcendentals=0),
        name="front",
    )(targets, pairs, split, interp, cols, rows, inverse)


def rest_kernel(targets, pairs, split, interp_h, cols_h, rows_h, inverse_h, self_h, start_h,
                edge_out, partner_out, total_out, coarse_out, skel_out,
                interp, cols, rows, inverse, self_block, w_far, compressor, grams, start, acc, skel, in_sems, out_sems):
    copies = input_copies((interp_h, cols_h, rows_h, inverse_h, self_h), (interp, cols, rows, inverse, self_block), in_sems)
    start_copy = pltpu.make_async_copy(start_h, start, out_sems.at[5])
    for copy in copies[0]:
        copy.start()
    start_copy.start()
    for copy in copies[1]:
        copy.start()

    def clear(n, _):
        acc[n] = jnp.zeros((SK, SK), F32)
        return 0

    lax.fori_loop(0, 2 * SLOTS, clear, 0)
    start_copy.wait()

    def widen(n, _):
        acc[2 * SLOTS + n] = start[n].astype(F32)
        return 0

    lax.fori_loop(0, SLOTS, widen, 0)
    parity = lax.rem(lax.axis_index("box"), 2)

    for box in range(BOXES):
        pick_skel = products(box, copies[box], split, interp, inverse, rows, cols, w_far, compressor, grams)

        def add(n, _):
            pair = lax.div(n, 2)
            side = lax.rem(n, 2)
            away, slot = relation(targets, box, pair, side)

            @pl.when((away <= 1) & (away >= -1))
            def _():
                place = slot + jnp.where(away == 0, 2 * SLOTS, jnp.where(away == 1, 0, SLOTS))
                acc[place] = acc[place] - grams[pairs[box, side, pair], pairs[box, 1 - side, pair]]

            return 0

        lax.fori_loop(0, 2 * PAIRS, add, 0)
        copies[box][4].wait()
        x_self = mul(self_block[box], compressor[...]).astype(BF16)
        y_self = mul(x_self, inverse[box]).astype(BF16)
        pick_rows = pick_skel.astype(F32).T.astype(BF16)
        for n in range(ROWS // TILE):
            at = slice(n * TILE, (n + 1) * TILE)
            base = lax.dot_general(pick_rows, cols[box, at, :], NT, preferred_element_type=F32)
            base = base - lax.dot_general(y_self, w_far[at, :], NT, preferred_element_type=F32)
            for k in range(TILE // SK):
                j = n * (TILE // SK) + k
                skel[j // 4, box, j % 4] = base[:, k * SK:(k + 1) * SK]

    outs = [
        pltpu.make_async_copy(acc.at[pl.ds(0, SLOTS)], edge_out, out_sems.at[0]),
        pltpu.make_async_copy(acc.at[pl.ds(SLOTS, SLOTS)], partner_out, out_sems.at[1]),
        pltpu.make_async_copy(acc.at[pl.ds(2 * SLOTS, SLOTS)], total_out, out_sems.at[2]),
        pltpu.make_async_copy(skel.at[parity], coarse_out.at[pl.ds(2 * parity, 2)], out_sems.at[3]),
        pltpu.make_async_copy(skel.at[1 - parity], skel_out, out_sems.at[4]),
    ]
    for copy in outs:
        copy.start()
    for copy in outs:
        copy.wait()


def rest(targets, pairs, split, interp, cols, rows, inverse, self_block, start):
    scratch = box_scratch()
    scratch.insert(4, pltpu.VMEM((BOXES, SK, P_SIZE), BF16))
    return pl.pallas_call(
        rest_kernel,
        out_shape=(
            block_type(SLOTS), block_type(SLOTS), block_type(SLOTS),
            jax.ShapeDtypeStruct((2 * BOXES, NB // 2, SK, SK), F32),
            jax.ShapeDtypeStruct((BOXES, NB // 2, SK, SK), F32),
        ),
        in_specs=[SMEM, SMEM, VMEM] + [ANY] * 6,
        out_specs=(ANY,) * 5,
        scratch_shapes=scratch + [
            pltpu.VMEM((SLOTS, SK, SK), BF16),
            pltpu.VMEM((3 * SLOTS, SK, SK), F32),
            pltpu.VMEM((2, BOXES, NB // 2, SK, SK), F32),
            pltpu.SemaphoreType.DMA((BOXES, 5)),
            pltpu.SemaphoreType.DMA((6,)),
        ],
        compiler_params=pltpu.CompilerParams(vmem_limit_bytes=VMEM_BYTES),
        cost_estimate=pl.CostEstimate(flops=4_400_000_000, bytes_accessed=20_000_000, transcendentals=0),
        name="rest",
    )(targets, pairs, split, interp, cols, rows, inverse, self_block, start)


def merge_kernel(ids, edge, arrived, first, second):
    first[...] = edge[:FIRST]
    second[...] = edge[FIRST:]

    def add(n, _):
        slot = ids[n]

        @pl.when((slot >= 0) & (slot < FIRST))
        def _():
            first[slot] = first[slot] + arrived[n]

        @pl.when(slot >= FIRST)
        def _():
            second[slot - FIRST] = second[slot - FIRST] + arrived[n]

        return 0

    lax.fori_loop(0, CAP, add, 0)


def merge(ids, edge, arrived):
    return pl.pallas_call(
        merge_kernel,
        out_shape=(block_type(FIRST), block_type(SLOTS - FIRST)),
        in_specs=[SMEM, VMEM, VMEM],
        out_specs=(VMEM, VMEM),
        compiler_params=pltpu.CompilerParams(vmem_limit_bytes=VMEM_BYTES),
        cost_estimate=pl.CostEstimate(flops=1_000_000, bytes_accessed=9_000_000, transcendentals=0),
        name="merge",
    )(ids, edge, arrived)


def add_compact_kernel(ids, total, partner, arrived, out):
    out[...] = total[...] + partner[...]

    def add(n, _):
        slot = ids[n]

        @pl.when(slot >= 0)
        def _():
            out[slot] = out[slot] + arrived[n]

        return 0

    lax.fori_loop(0, CAP, add, 0)


def add_compact(ids, total, partner, arrived):
    return pl.pallas_call(
        add_compact_kernel,
        out_shape=block_type(SLOTS),
        in_specs=[SMEM, VMEM, VMEM, VMEM],
        out_specs=VMEM,
        compiler_params=pltpu.CompilerParams(vmem_limit_bytes=VMEM_BYTES),
        cost_estimate=pl.CostEstimate(flops=2_000_000, bytes_accessed=12_000_000, transcendentals=0),
        name="add_compact",
    )(ids, total, partner, arrived)


def add_dense_kernel(total, arrived, out):
    out[...] = total[...] + arrived[...]


def add_dense(total, arrived, begin, step):
    count = arrived.shape[0]
    here = pl.BlockSpec((step, SK, SK), lambda n: (n + begin // step, 0, 0))
    return pl.pallas_call(
        add_dense_kernel,
        out_shape=block_type(SLOTS),
        grid=(count // step,),
        in_specs=[here, pl.BlockSpec((step, SK, SK), lambda n: (n, 0, 0))],
        out_specs=here,
        input_output_aliases={0: 0},
        cost_estimate=pl.CostEstimate(flops=1_000_000, bytes_accessed=count * 3 * 65536, transcendentals=0),
        name="add_dense",
    )(total, arrived)


def place_kernel(coarse, received, out, sem):
    parity = lax.rem(lax.axis_index("box"), 2)
    copy = pltpu.make_async_copy(received, out.at[pl.ds(2 - 2 * parity, 2)], sem)
    copy.start()
    copy.wait()


def place(coarse, received):
    return pl.pallas_call(
        place_kernel,
        out_shape=jax.ShapeDtypeStruct(coarse.shape, F32),
        in_specs=[ANY, ANY],
        out_specs=ANY,
        scratch_shapes=[pltpu.SemaphoreType.DMA],
        input_output_aliases={0: 0},
        cost_estimate=pl.CostEstimate(flops=0, bytes_accessed=1_000_000, transcendentals=0),
        name="place",
    )(coarse, received)


def moved(value, route):
    devices = lax.axis_size("box")
    return lax.ppermute(value, "box", [(i, route(i) % devices) for i in range(devices)])


def other_core(i):
    return i ^ 1


def across(i):
    return i + 1 if i % 2 else i - 1


def beyond(i):
    return i + 2 if i % 2 else i - 2


def body(self_block, interp, split, inverse_block, row_blocks, col_blocks, pairs, targets, pair_blocks):
    targets = jnp.transpose(targets, (0, 2, 1))
    pairs = jnp.transpose(pairs, (0, 2, 1))
    rows = row_blocks.reshape(BOXES, ROWS, P_SIZE)
    cols = col_blocks.reshape(BOXES, ROWS, P_SIZE)
    near, near_ids, far, far_ids = front(targets, pairs, split, interp, cols, rows, inverse_block)
    near, near_ids = moved((near, near_ids), beyond)
    far, far_ids = moved((far, far_ids), other_core)
    edge, partner, total, coarse, skel = rest(
        targets, pairs, split, interp, cols, rows, inverse_block, self_block, pair_blocks
    )
    first, second = merge(far_ids, edge, far)
    first = moved(first, across)
    second = moved(second, across)
    partner = moved(partner, other_core)
    skel = moved(skel, other_core)
    coarse = place(coarse, skel)
    total = add_compact(near_ids, total, partner, near)
    total = add_dense(total, first, 0, 8)
    total = add_dense(total, second, FIRST, 4)
    return total, coarse[None]


def solution(mesh):
    return jax.shard_map(
        body,
        mesh=mesh,
        in_specs=(
            P("box", None, None),
            P("box", None, None),
            P("box", None),
            P("box", None, None),
            P("box", None, None, None),
            P("box", None, None, None),
            P("box", None, None),
            P("box", None, None),
            P("box", None, None),
        ),
        out_specs=(P("box", None, None), P("box", None, None, None, None)),
        check_vma=False,
    )
```

profile of v0, /device:TPU:0, one launch (start us, length us, event | category | flops | bytes accessed | tf_op | source)
XLA Modules:
  0.0 125.4 jit_solution(2726562714250389882)
XLA Ops:
  0.6 0.0 copy-start.3
  0.6 1.1 copy-done.3
  1.7 0.0 copy-start.5
  1.7 0.9 copy-done.5
  2.6 0.0 copy-start.6
  2.6 0.7 copy-done.6
  3.3 0.0 copy-start.7
  3.3 0.7 copy-done.7
  4.0 0.0 copy-start.8
  4.0 0.7 copy-done.8
  4.7 0.0 copy-start.1
  4.7 0.0 copy-start.2
  4.7 0.0 copy-start.4
  4.7 19.9 %front.1 = (f32[32,128,128]{2,1,0:T(8,128)}, s32[32]{0:T(128)S(1)}, f32[32,128,128]{2,1,0:T(8,128)S(1)}, s32[32]{0:T(128)S(1)}) custom-call(s32[2,2,24]{2,1,0:T(2,128)S(1)} %bitcast.7, s32[2,2,24]{2,1,0:T(2,128)S(1)} %bitcast.9, s32[2,512]{1,0:T(2,128)S(1)} %copy-done.6, bf16[2,384,128]{2,1,0:T(8,128)(2,1)S(1)} %copy-done.5, bf16[2,1024,512]{2,1,0:T(8,128)(2,1)} %bitcast.5, ...), custom_call_target="tpu_custom_call" | custom-call | flops 4000000000 | bytes 10000000 | tf_op jit(solution)/shard_map/front/pallas_call | solution.py:180
  24.6 0.1 collective-permute-start.4
  24.7 0.0 copy-done.1
  24.7 0.0 copy-done.2
  24.7 0.0 copy-done.4
  24.7 20.6 %rest.1 = (f32[48,128,128]{2,1,0:T(8,128)}, f32[48,128,128]{2,1,0:T(8,128)}, f32[48,128,128]{2,1,0:T(8,128)}, f32[4,4,128,128]{3,2,1,0:T(8,128)}, f32[2,4,128,128]{3,2,1,0:T(8,128)S(1)}) custom-call(s32[2,2,24]{2,1,0:T(2,128)S(1)} %bitcast.8, s32[2,2,24]{2,1,0:T(2,128)S(1)} %bitcast.10, s32[2,512]{1,0:T(2,128)S(1)} %copy-done.6, ...), custom_call_target="tpu_custom_call" | custom-call | flops 4400000000 | bytes 20000000 | tf_op jit(solution)/shard_map/rest/pallas_call | solution.py:266
  45.3 0.6 collective-permute-start.1
  45.9 0.1 collective-permute-start.3
  46.0 9.0 %collective-permute-start.2 = (f32[32,128,128]{2,1,0:T(8,128)}, f32[32,128,128]{2,1,0:T(8,128)}, u32[]{:S(2)}, u32[]{:S(2)}) collective-permute-start(f32[32,128,128]{2,1,0:T(8,128)} %get-tuple-element.16), channel_id=1, source_target_pairs={{0,126},{1,3},{2,0},{3,5},{4,2},{5,7},{6,4},{7,9},{8,6},{9,11},{10... | collective-permute-start | bytes 6291464 | tf_op jit(solution)/shard_map/ppermute | solution.py:388
  55.0 0.0 collective-permute-done.3.ids
  55.0 0.0 collective-permute-done.4.arrived
  55.0 0.0 copy-start
  55.0 4.5 %merge.1 = (f32[32,128,128]{2,1,0:T(8,128)}, f32[16,128,128]{2,1,0:T(8,128)}) custom-call(s32[32]{0:T(128)S(1)} %collective-permute-done.3.ids, f32[48,128,128]{2,1,0:T(8,128)} %get-tuple-element.18.edge, f32[32,128,128]{2,1,0:T(8,128)S(1)} %collective-permute-done.4.arrived), custom_call_target="tpu_custom_call" | custom-call | flops 1000000 | bytes 9000000 | tf_op jit(solution)/shard_map/merge/pallas_call | solution.py:309
  59.5 4.8 %collective-permute-start.5 = (f32[32,128,128]{2,1,0:T(8,128)}, f32[32,128,128]{2,1,0:T(8,128)}, u32[]{:S(2)}, u32[]{:S(2)}) collective-permute-start(f32[32,128,128]{2,1,0:T(8,128)} %get-tuple-element.20), channel_id=1, source_target_pairs={{0,127},{1,2},{2,1},{3,4},{4,3},{5,6},{6,5},{7,8},{8,7},{9,10},{10... | collective-permute-start | bytes 6291464 | tf_op jit(solution)/shard_map/ppermute | solution.py:388
  64.4 2.3 %collective-permute-start.6 = (f32[16,128,128]{2,1,0:T(8,128)}, f32[16,128,128]{2,1,0:T(8,128)}, u32[]{:S(2)}, u32[]{:S(2)}) collective-permute-start(f32[16,128,128]{2,1,0:T(8,128)} %get-tuple-element.21), channel_id=1, source_target_pairs={{0,127},{1,2},{2,1},{3,4},{4,3},{5,6},{6,5},{7,8},{8,7},{9,10},{10... | collective-permute-start | bytes 3145736 | tf_op jit(solution)/shard_map/ppermute | solution.py:388
  66.7 0.0 collective-permute-start.7
  66.7 1.9 %collective-permute-done.7.received = f32[2,4,128,128]{3,2,1,0:T(8,128)S(1)} collective-permute-done((f32[2,4,128,128]{3,2,1,0:T(8,128)S(1)}, f32[2,4,128,128]{3,2,1,0:T(8,128)S(1)}, u32[]{:S(2)}, u32[]{:S(2)}) %collective-permute-start.7) | collective-permute-done | bytes 524320 | tf_op jit(solution)/shard_map/ppermute | solution.py:388
  68.6 0.0 copy-start.9
  68.6 4.9 %collective-permute-start = (s32[32]{0:T(128)S(1)}, s32[32]{0:T(128)S(1)}, u32[]{:S(2)}, u32[]{:S(2)}) collective-permute-start(s32[32]{0:T(128)S(1)} %get-tuple-element.13), channel_id=1, source_target_pairs={{0,126},{1,3},{2,0},{3,5},{4,2},{5,7},{6,4},{7,9},{8,6},{9,11},{10... | collective-permute-start | bytes 392 | tf_op jit(solution)/shard_map/ppermute | solution.py:388
  73.5 0.0 copy-done.9
  73.5 17.0 %place.1 = f32[4,4,128,128]{3,2,1,0:T(8,128)} custom-call(f32[4,4,128,128]{3,2,1,0:T(8,128)} %get-tuple-element.22.coarse, f32[2,4,128,128]{3,2,1,0:T(8,128)} %copy-done.9), custom_call_target="tpu_custom_call", output_to_operand_aliasing={{}: (0, {})} | custom-call | bytes 1000000 | tf_op jit(solution)/shard_map/place/pallas_call | solution.py:374
  90.5 22.1 %collective-permute-done.ids = s32[32]{0:T(128)S(1)} collective-permute-done((s32[32]{0:T(128)S(1)}, s32[32]{0:T(128)S(1)}, u32[]{:S(2)}, u32[]{:S(2)}) %collective-permute-start) | collective-permute-done | bytes 160 | tf_op jit(solution)/shard_map/ppermute | solution.py:388
  112.5 0.0 collective-permute-done.2.arrived
  112.5 0.0 collective-permute-done.1.partner
  112.5 0.0 copy-done
  112.5 5.1 %add_compact.1.total = f32[48,128,128]{2,1,0:T(8,128)} custom-call(s32[32]{0:T(128)S(1)} %collective-permute-done.ids, f32[48,128,128]{2,1,0:T(8,128)S(1)} %copy-done, f32[48,128,128]{2,1,0:T(8,128)} %collective-permute-done.1.partner, f32[32,128,128]{2,1,0:T(8,128)} %collective-permute-done.2.arrived), custom_call_target="tpu_custom_call" | custom-call | flops 2000000 | bytes 12000000 | tf_op jit(solution)/shard_map/add_compact/pallas_call | solution.py:336
  117.6 0.0 collective-permute-done.5.arrived
  117.6 4.2 %add_dense.2.total = f32[48,128,128]{2,1,0:T(8,128)} custom-call(f32[48,128,128]{2,1,0:T(8,128)} %add_compact.1.total, f32[32,128,128]{2,1,0:T(8,128)} %collective-permute-done.5.arrived), custom_call_target="tpu_custom_call", output_to_operand_aliasing={{}: (0, {})} | custom-call | flops 1000000 | bytes 6291456 | tf_op jit(solution)/shard_map/add_dense/pallas_call | solution.py:354
  121.8 0.0 collective-permute-done.6.arrived
  121.8 3.6 %add_dense.3 = f32[48,128,128]{2,1,0:T(8,128)} custom-call(f32[48,128,128]{2,1,0:T(8,128)} %add_dense.2.total, f32[16,128,128]{2,1,0:T(8,128)} %collective-permute-done.6.arrived), custom_call_target="tpu_custom_call", output_to_operand_aliasing={{}: (0, {})} | custom-call | flops 1000000 | bytes 3145728 | tf_op jit(solution)/shard_map/add_dense/pallas_call | solution.py:354
Async XLA Ops:
  0.6 1.1 copy-start.3
  1.7 0.9 copy-start.5
  2.6 0.7 copy-start.6
  3.3 0.7 copy-start.7
  4.0 0.7 copy-start.8
  4.7 20.0 %copy-start.1 = (bf16[2,8,128,512]{3,2,1,0:T(8,128)(2,1)S(1)}, bf16[2,8,128,512]{3,2,1,0:T(8,128)(2,1)}, u32[]{:S(2)}) copy-start(bf16[2,8,128,512]{3,2,1,0:T(8,128)(2,1)} %param.14) | copy-start | bytes 6291460
  4.7 20.0 %copy-start.2 = (bf16[48,128,128]{2,1,0:T(8,128)(2,1)S(1)}, bf16[48,128,128]{2,1,0:T(8,128)(2,1)}, u32[]{:S(2)}) copy-start(bf16[48,128,128]{2,1,0:T(8,128)(2,1)} %start_h.1) | copy-start | bytes 4718596
  4.7 20.0 %copy-start.4 = (bf16[2,128,512]{2,1,0:T(8,128)(2,1)S(1)}, bf16[2,128,512]{2,1,0:T(8,128)(2,1)}, u32[]{:S(2)}) copy-start(bf16[2,128,512]{2,1,0:T(8,128)(2,1)} %self_h.1) | copy-start | bytes 786436
  24.6 30.4 %collective-permute-start.4 = (f32[32,128,128]{2,1,0:T(8,128)S(1)}, f32[32,128,128]{2,1,0:T(8,128)S(1)}, u32[]{:S(2)}, u32[]{:S(2)}) collective-permute-start(f32[32,128,128]{2,1,0:T(8,128)S(1)} %get-tuple-element.19), channel_id=1, source_target_pairs={{0,1},{1,0},{2,3},{3,2},{4,5},{5,4},{6,7},{7,6},{8,9},{9,8},{10,11... | collective-permute-start | bytes 6291464 | tf_op jit(solution)/shard_map/ppermute | solution.py:388
  45.3 67.3 %collective-permute-start.1 = (f32[48,128,128]{2,1,0:T(8,128)}, f32[48,128,128]{2,1,0:T(8,128)}, u32[]{:S(2)}, u32[]{:S(2)}) collective-permute-start(f32[48,128,128]{2,1,0:T(8,128)} %get-tuple-element.15), channel_id=1, source_target_pairs={{0,1},{1,0},{2,3},{3,2},{4,5},{5,4},{6,7},{7,6},{8,9},{9,8},{10,11... | collective-permute-start | bytes 9437192 | tf_op jit(solution)/shard_map/ppermute | solution.py:388
  45.9 9.1 %collective-permute-start.3 = (s32[32]{0:T(128)S(1)}, s32[32]{0:T(128)S(1)}, u32[]{:S(2)}, u32[]{:S(2)}) collective-permute-start(s32[32]{0:T(128)S(1)} %get-tuple-element.17), channel_id=1, source_target_pairs={{0,1},{1,0},{2,3},{3,2},{4,5},{5,4},{6,7},{7,6},{8,9},{9,8},{10,11... | collective-permute-start | bytes 392 | tf_op jit(solution)/shard_map/ppermute | solution.py:388
  46.0 66.5 %collective-permute-start.2 = (f32[32,128,128]{2,1,0:T(8,128)}, f32[32,128,128]{2,1,0:T(8,128)}, u32[]{:S(2)}, u32[]{:S(2)}) collective-permute-start(f32[32,128,128]{2,1,0:T(8,128)} %get-tuple-element.16), channel_id=1, source_target_pairs={{0,126},{1,3},{2,0},{3,5},{4,2},{5,7},{6,4},{7,9},{8,6},{9,11},{10... | collective-permute-start | bytes 6291464 | tf_op jit(solution)/shard_map/ppermute | solution.py:388
  55.0 57.6 %copy-start = (f32[48,128,128]{2,1,0:T(8,128)S(1)}, f32[48,128,128]{2,1,0:T(8,128)}, u32[]{:S(2)}) copy-start(f32[48,128,128]{2,1,0:T(8,128)} %get-tuple-element.14.total) | copy-start | bytes 9437188
  59.5 58.1 %collective-permute-start.5 = (f32[32,128,128]{2,1,0:T(8,128)}, f32[32,128,128]{2,1,0:T(8,128)}, u32[]{:S(2)}, u32[]{:S(2)}) collective-permute-start(f32[32,128,128]{2,1,0:T(8,128)} %get-tuple-element.20), channel_id=1, source_target_pairs={{0,127},{1,2},{2,1},{3,4},{4,3},{5,6},{6,5},{7,8},{8,7},{9,10},{10... | collective-permute-start | bytes 6291464 | tf_op jit(solution)/shard_map/ppermute | solution.py:388
  64.4 57.4 %collective-permute-start.6 = (f32[16,128,128]{2,1,0:T(8,128)}, f32[16,128,128]{2,1,0:T(8,128)}, u32[]{:S(2)}, u32[]{:S(2)}) collective-permute-start(f32[16,128,128]{2,1,0:T(8,128)} %get-tuple-element.21), channel_id=1, source_target_pairs={{0,127},{1,2},{2,1},{3,4},{4,3},{5,6},{6,5},{7,8},{8,7},{9,10},{10... | collective-permute-start | bytes 3145736 | tf_op jit(solution)/shard_map/ppermute | solution.py:388
  66.7 1.9 %collective-permute-start.7 = (f32[2,4,128,128]{3,2,1,0:T(8,128)S(1)}, f32[2,4,128,128]{3,2,1,0:T(8,128)S(1)}, u32[]{:S(2)}, u32[]{:S(2)}) collective-permute-start(f32[2,4,128,128]{3,2,1,0:T(8,128)S(1)} %get-tuple-element.23), channel_id=1, source_target_pairs={{0,1},{1,0},{2,3},{3,2},{4,5},{5,4},{6,7},{7,6},{8,9},{9,8},{10,11... | collective-permute-start | bytes 1572872 | tf_op jit(solution)/shard_map/ppermute | solution.py:388
  68.6 4.9 %copy-start.9 = (f32[2,4,128,128]{3,2,1,0:T(8,128)}, f32[2,4,128,128]{3,2,1,0:T(8,128)S(1)}, u32[]{:S(2)}) copy-start(f32[2,4,128,128]{3,2,1,0:T(8,128)S(1)} %collective-permute-done.7.received) | copy-start | bytes 1572868
  68.6 43.9 %collective-permute-start = (s32[32]{0:T(128)S(1)}, s32[32]{0:T(128)S(1)}, u32[]{:S(2)}, u32[]{:S(2)}) collective-permute-start(s32[32]{0:T(128)S(1)} %get-tuple-element.13), channel_id=1, source_target_pairs={{0,126},{1,3},{2,0},{3,5},{4,2},{5,7},{6,4},{7,9},{8,6},{9,11},{10... | collective-permute-start | bytes 392 | tf_op jit(solution)/shard_map/ppermute | solution.py:388
where the time goes:
time: 127 us; the launch traced here: 125 us
  Pallas kernels  74.8 us (59%)
  waiting for transfers between devices  24 us (19%)
  starting transfers between devices  21.8 us (17%)
  local copies, waits for them, and re-layouts  4.05 us (3%)
    ppermute x8, waiting for transfers between devices, moved(): lax.ppermute(value, 'box', [(i, route(i) % devices) for i in range(device...  24 us
    ppermute x8, starting transfers between devices, moved(): lax.ppermute(value, 'box', [(i, route(i) % devices) for i in range(device...  21.8 us
    pallas_call x1, Pallas kernels, rest(): pl.pallas_call(rest_kernel, out_shape=(block_type(SLOTS), block_type(SLOT...  20.6 us
    pallas_call x1, Pallas kernels, front(): pl.pallas_call(front_kernel, out_shape=(block_type(CAP), ids_type(CAP), b...  19.9 us
    pallas_call x1, Pallas kernels, place(): pl.pallas_call(place_kernel, out_shape=jax.ShapeDtypeStruct(coarse.shape,...  17 us
    pallas_call x2, Pallas kernels, add_dense(): pl.pallas_call(add_dense_kernel, out_shape=block_type(SLOTS), grid=(count...  7.74 us
    pallas_call x1, Pallas kernels, add_compact(): pl.pallas_call(add_compact_kernel, out_shape=block_type(SLOTS), in_specs=...  5.07 us
    pallas_call x1, Pallas kernels, merge(): pl.pallas_call(merge_kernel, out_shape=(block_type(FIRST), block_type(SLO...  4.55 us
  transfers between devices with their start and end apart: 8, of which 2 were waited for; matrix products, arithmetic and copies ran while one was open for 0% of the time, Pallas kernels for 41%

commit v1 on v0

v1 whole, which is shorter than its diff:
```python
import functools

import jax
import jax.numpy as jnp
from jax import lax
from jax.experimental import pallas as pl
from jax.experimental.pallas import tpu as pltpu
from jax.sharding import PartitionSpec as P

P_SIZE = 512
SK = 128
RD = 384
BOXES = 2
NB = 8
PAIRS = 24
SLOTS = 48
CAP = 32
ROWS = NB * SK
TILE = 512
FIRST = 32
VMEM_BYTES = 62 * 1024 * 1024
F32 = jnp.float32
BF16 = jnp.bfloat16
NT = (((1,), (1,)), ((), ()))

ANY = pl.BlockSpec(memory_space=pl.ANY)
VMEM = pl.BlockSpec(memory_space=pltpu.VMEM)


def block_type(count):
    return jax.ShapeDtypeStruct((count, SK, SK), F32)


def cost(us):
    return pl.CostEstimate(flops=us * 1_000_000_000, bytes_accessed=0, transcendentals=0)


def payload_type(count):
    return jax.ShapeDtypeStruct((count * SK + 8, SK), F32)


def input_copies(hbm, vmem, sems):
    out = []
    for box in range(BOXES):
        out.append([
            pltpu.make_async_copy(source.at[box], target.at[box], sems.at[box, n])
            for n, (source, target) in enumerate(zip(hbm, vmem))
        ])
    return out


def compressor_of(split, interp, box):
    points = lax.broadcasted_iota(jnp.int32, (P_SIZE, RD), 0)
    pick_red = points == split[box:box + 1, :RD]
    points = lax.broadcasted_iota(jnp.int32, (P_SIZE, SK), 0)
    pick_skel = (points == split[box:box + 1, RD:]).astype(F32).astype(BF16)
    spread = lax.dot_general(pick_skel, interp[box], NT, preferred_element_type=F32)
    return (jnp.where(pick_red, 1.0, 0.0) - spread).astype(BF16), pick_skel


def mul(a, b):
    return jnp.dot(a, b, preferred_element_type=F32)


def products(box, copies, split, interp, inverse, rows, cols, w_far, y_near, compressor, grams):
    copies[0].wait()
    comp, pick_skel = compressor_of(split, interp, box)
    compressor[...] = comp
    copies[1].wait()

    def far(n, _):
        at = pl.ds(pl.multiple_of(n * TILE, TILE), TILE)
        w_far[at, :] = mul(cols[box, at, :], compressor[...]).astype(BF16)
        return 0

    lax.fori_loop(0, ROWS // TILE, far, 0, unroll=True)
    copies[2].wait()
    copies[3].wait()

    def near(n, _):
        at = pl.ds(pl.multiple_of(n * TILE, TILE), TILE)
        x_near = mul(rows[box, at, :], compressor[...]).astype(BF16)
        y_near[at, :] = mul(x_near, inverse[box]).astype(BF16)
        return 0

    lax.fori_loop(0, ROWS // TILE, near, 0, unroll=True)

    def gram(n, _):
        at = pl.ds(pl.multiple_of(n * TILE, TILE), TILE)
        tile = lax.dot_general(y_near[...], w_far[at, :], NT, preferred_element_type=F32)
        for i in range(NB):
            for k in range(TILE // SK):
                grams[i, n * (TILE // SK) + k] = tile[i * SK:(i + 1) * SK, k * SK:(k + 1) * SK]
        return 0

    lax.fori_loop(0, ROWS // TILE, gram, 0, unroll=True)
    return pick_skel


def front_kernel(targets_h, pairs_h, split, interp_h, cols_h, rows_h, inverse_h, near_out, far_out,
                 interp, cols, rows, inverse, w_far, y_near, compressor, grams, acc, targets, pairs, used, todo, near_ids, far_ids, in_sems, out_sems, small_sems):
    small = [
        pltpu.make_async_copy(targets_h, targets, small_sems.at[0]),
        pltpu.make_async_copy(pairs_h, pairs, small_sems.at[1]),
    ]
    for copy in small:
        copy.start()
    copies = input_copies((interp_h, cols_h, rows_h, inverse_h), (interp, cols, rows, inverse), in_sems)
    for box in range(BOXES):
        for copy in copies[box]:
            copy.start()

    def clear_used(n, _):
        used[n] = 0
        return 0

    lax.fori_loop(0, 2 * SLOTS, clear_used, 0, unroll=8)
    device = lax.axis_index("box")
    odd = lax.rem(device, 2)
    all_slots = lax.axis_size("box") * SLOTS
    here = device * SLOTS
    for copy in small:
        copy.wait()

    ends = []
    for box in range(BOXES):

        def enter(pair, end):
            numbers = [pairs[box, 0, pair], pairs[box, 1, pair]]
            for side in range(2):
                away = targets[box, side, pair] - here
                away = jnp.where(away >= all_slots // 2, away - all_slots, away)
                away = jnp.where(away < -(all_slots // 2), away + all_slots, away)
                ahead = away >= 2 * SLOTS
                wanted = ahead | (away < -SLOTS)
                slot = jnp.where(ahead, away - 2 * SLOTS, away + 2 * SLOTS)
                near = ahead.astype(jnp.int32) == odd
                place = jnp.where(wanted, jnp.where(near, slot, slot + SLOTS), 2 * SLOTS)
                todo[box, end] = place * 128 + numbers[side] * 16 + numbers[1 - side] * 2 + used[place]
                used[place] = 1
                end = end + wanted.astype(jnp.int32)
            return end

        ends.append(lax.fori_loop(0, PAIRS, enter, jnp.int32(0), unroll=2))

    def number(n, counts):
        out = []
        for base, ids, count in ((0, near_ids, counts[0]), (SLOTS, far_ids, counts[1])):
            ids[0, count] = n.astype(F32)
            out.append(count + used[base + n])
        return tuple(out)

    counts = lax.fori_loop(0, SLOTS, number, (jnp.int32(0), jnp.int32(0)), unroll=4)
    for ids, count in ((near_ids, counts[0]), (far_ids, counts[1])):

        def blank(n, _):
            ids[0, n] = -1.0
            return 0

        lax.fori_loop(count, CAP, blank, 0)

    for box in range(BOXES):
        products(box, copies[box], split, interp, inverse, rows, cols, w_far, y_near, compressor, grams)

        def add(n, _):
            entry = todo[box, n]
            place = lax.shift_right_logical(entry, 7)
            i = lax.shift_right_logical(entry, 4) & 7
            j = lax.shift_right_logical(entry, 1) & 7
            before = acc[place]
            acc[place] = jnp.where((entry & 1) == 1, before, 0.0) - grams[i, j]
            return 0

        lax.fori_loop(0, ends[box], add, 0)

    labels = [
        pltpu.make_async_copy(near_ids, near_out.at[pl.ds(CAP * SK, 8)], small_sems.at[0]),
        pltpu.make_async_copy(far_ids, far_out.at[pl.ds(CAP * SK, 8)], small_sems.at[1]),
    ]
    for copy in labels:
        copy.start()
    for base, out, ids, count in ((0, near_out, near_ids, counts[0]), (SLOTS, far_out, far_ids, counts[1])):

        def send(n, _):
            pltpu.make_async_copy(acc.at[base + ids[0, n].astype(jnp.int32)], out.at[pl.ds(pl.multiple_of(n * SK, SK), SK)], out_sems.at[base + n]).start()
            return 0

        lax.fori_loop(0, count, send, 0)

    for base, out, ids, count in ((0, near_out, near_ids, counts[0]), (SLOTS, far_out, far_ids, counts[1])):

        def drain(n, _):
            pltpu.make_async_copy(acc.at[base], out.at[pl.ds(0, SK)], out_sems.at[base + n]).wait()
            return 0

        lax.fori_loop(0, count, drain, 0)

    for copy in labels:
        copy.wait()


def box_scratch():
    return [
        pltpu.VMEM((BOXES, RD, SK), BF16),
        pltpu.VMEM((BOXES, ROWS, P_SIZE), BF16),
        pltpu.VMEM((BOXES, ROWS, P_SIZE), BF16),
        pltpu.VMEM((BOXES, RD, RD), BF16),
        pltpu.VMEM((ROWS, RD), BF16),
        pltpu.VMEM((ROWS, RD), BF16),
        pltpu.VMEM((P_SIZE, RD), BF16),
        pltpu.VMEM((NB, NB, SK, SK), F32),
    ]


def front(targets, pairs, split, interp, cols, rows, inverse):
    return pl.pallas_call(
        front_kernel,
        out_shape=(payload_type(CAP), payload_type(CAP)),
        in_specs=[ANY, ANY, VMEM, ANY, ANY, ANY, ANY],
        out_specs=(ANY, ANY),
        scratch_shapes=box_scratch() + [
            pltpu.VMEM((2 * SLOTS, SK, SK), F32),
            pltpu.SMEM((BOXES, 2, PAIRS), jnp.int32),
            pltpu.SMEM((BOXES, 2, PAIRS), jnp.int32),
            pltpu.SMEM((2 * SLOTS + 1,), jnp.int32),
            pltpu.SMEM((BOXES, 2 * PAIRS + 1), jnp.int32),
            pltpu.SMEM((8, 128), F32),
            pltpu.SMEM((8, 128), F32),
            pltpu.SemaphoreType.DMA((BOXES, 4)),
            pltpu.SemaphoreType.DMA((2 * SLOTS,)),
            pltpu.SemaphoreType.DMA((2,)),
        ],
        compiler_params=pltpu.CompilerParams(vmem_limit_bytes=VMEM_BYTES),
        cost_estimate=cost(1),
        name="front",
    )(targets, pairs, split, interp, cols, rows, inverse)


def rest_kernel(targets_h, pairs_h, split, interp_h, cols_h, rows_h, inverse_h, start_h,
                edge_out, partner_out, total_out,
                interp, cols, rows, inverse, w_far, y_near, compressor, grams, start, acc, targets, pairs, todo,
                in_sems, out_sems, small_sems):
    small = [
        pltpu.make_async_copy(targets_h, targets, small_sems.at[0]),
        pltpu.make_async_copy(pairs_h, pairs, small_sems.at[1]),
    ]
    for copy in small:
        copy.start()
    copies = input_copies((interp_h, cols_h, rows_h, inverse_h), (interp, cols, rows, inverse), in_sems)
    start_copy = pltpu.make_async_copy(start_h, start, out_sems.at[3])
    for copy in copies[0]:
        copy.start()
    start_copy.start()
    for copy in copies[1]:
        copy.start()

    def clear(n, _):
        acc[n] = jnp.zeros((SK, SK), F32)
        return 0

    lax.fori_loop(0, 2 * SLOTS, clear, 0)
    device = lax.axis_index("box")
    odd = lax.rem(device, 2)
    all_slots = lax.axis_size("box") * SLOTS
    here = device * SLOTS
    for copy in small:
        copy.wait()

    def enter(pair, ends):
        out = []
        for box in range(BOXES):
            end = ends[box]
            numbers = [pairs[box, 0, pair], pairs[box, 1, pair]]
            for side in range(2):
                away = targets[box, side, pair] - here
                away = jnp.where(away >= all_slots // 2, away - all_slots, away)
                away = jnp.where(away < -(all_slots // 2), away + all_slots, away)
                ahead = away >= SLOTS
                behind = away < 0
                wanted = (away < 2 * SLOTS) & (away >= -SLOTS)
                edge = ahead.astype(jnp.int32) == odd
                place = jnp.where(
                    ahead | behind,
                    jnp.where(ahead, away - SLOTS, away + SLOTS) + jnp.where(edge, 0, SLOTS),
                    away + 2 * SLOTS,
                )
                todo[box, end] = place * 64 + numbers[side] * 8 + numbers[1 - side]
                end = end + wanted.astype(jnp.int32)
            out.append(end)
        return tuple(out)

    ends = lax.fori_loop(0, PAIRS, enter, (jnp.int32(0), jnp.int32(0)))
    start_copy.wait()

    def widen(n, _):
        acc[2 * SLOTS + n] = start[n].astype(F32)
        return 0

    lax.fori_loop(0, SLOTS, widen, 0)
    for box in range(BOXES):
        products(box, copies[box], split, interp, inverse, rows, cols, w_far, y_near, compressor, grams)

        def add(n, _):
            entry = todo[box, n]
            place = lax.shift_right_logical(entry, 6)
            i = lax.shift_right_logical(entry, 3) & 7
            j = entry & 7
            acc[place] = acc[place] - grams[i, j]
            return 0

        lax.fori_loop(0, ends[box], add, 0)

    outs = [
        pltpu.make_async_copy(acc.at[pl.ds(0, SLOTS)], edge_out, out_sems.at[0]),
        pltpu.make_async_copy(acc.at[pl.ds(SLOTS, SLOTS)], partner_out, out_sems.at[1]),
        pltpu.make_async_copy(acc.at[pl.ds(2 * SLOTS, SLOTS)], total_out, out_sems.at[2]),
    ]
    for copy in outs:
        copy.start()
    for copy in outs:
        copy.wait()


def rest(targets, pairs, split, interp, cols, rows, inverse, start):
    return pl.pallas_call(
        rest_kernel,
        out_shape=(block_type(SLOTS), block_type(SLOTS), block_type(SLOTS)),
        in_specs=[ANY, ANY, VMEM] + [ANY] * 5,
        out_specs=(ANY,) * 3,
        scratch_shapes=box_scratch() + [
            pltpu.VMEM((SLOTS, SK, SK), BF16),
            pltpu.VMEM((3 * SLOTS, SK, SK), F32),
            pltpu.SMEM((BOXES, 2, PAIRS), jnp.int32),
            pltpu.SMEM((BOXES, 2, PAIRS), jnp.int32),
            pltpu.SMEM((BOXES, 2 * PAIRS + 1), jnp.int32),
            pltpu.SemaphoreType.DMA((BOXES, 4)),
            pltpu.SemaphoreType.DMA((4,)),
            pltpu.SemaphoreType.DMA((2,)),
        ],
        compiler_params=pltpu.CompilerParams(vmem_limit_bytes=VMEM_BYTES),
        cost_estimate=cost(1),
        name="rest",
    )(targets, pairs, split, interp, cols, rows, inverse, start)


def skeletons_kernel(after, split, interp_h, cols_h, inverse_h, self_h, coarse_out, skel_out,
                     interp, cols, inverse, self_block, w_far, skel, in_sems, out_sems):
    copies = input_copies((interp_h, cols_h, inverse_h, self_h), (interp, cols, inverse, self_block), in_sems)
    for box in range(BOXES):
        for copy in copies[box]:
            copy.start()
    parity = lax.rem(lax.axis_index("box"), 2)
    for box in range(BOXES):
        for copy in copies[box]:
            copy.wait()
        comp, pick_skel = compressor_of(split, interp, box)
        x_self = mul(self_block[box], comp).astype(BF16)
        y_self = mul(x_self, inverse[box]).astype(BF16)
        pick_rows = pick_skel.astype(F32).T.astype(BF16)
        w_far[...] = mul(cols[box], comp).astype(BF16)
        for n in range(ROWS // TILE):
            at = slice(n * TILE, (n + 1) * TILE)
            base = lax.dot_general(pick_rows, cols[box, at, :], NT, preferred_element_type=F32)
            base = base - lax.dot_general(y_self, w_far[at, :], NT, preferred_element_type=F32)
            for k in range(TILE // SK):
                j = n * (TILE // SK) + k
                skel[j // 4, box, j % 4] = base[:, k * SK:(k + 1) * SK]
    outs = [
        pltpu.make_async_copy(skel.at[parity], coarse_out.at[pl.ds(2 * parity, 2)], out_sems.at[0]),
        pltpu.make_async_copy(skel.at[1 - parity], skel_out, out_sems.at[1]),
    ]
    for copy in outs:
        copy.start()
    for copy in outs:
        copy.wait()


def skeletons(after, split, interp, cols, inverse, self_block):
    return pl.pallas_call(
        skeletons_kernel,
        out_shape=(
            jax.ShapeDtypeStruct((2 * BOXES, NB // 2, SK, SK), F32),
            jax.ShapeDtypeStruct((BOXES, NB // 2, SK, SK), F32),
        ),
        in_specs=[ANY, VMEM] + [ANY] * 4,
        out_specs=(ANY,) * 2,
        scratch_shapes=[
            pltpu.VMEM((BOXES, RD, SK), BF16),
            pltpu.VMEM((BOXES, ROWS, P_SIZE), BF16),
            pltpu.VMEM((BOXES, RD, RD), BF16),
            pltpu.VMEM((BOXES, SK, P_SIZE), BF16),
            pltpu.VMEM((ROWS, RD), BF16),
            pltpu.VMEM((2, BOXES, NB // 2, SK, SK), F32),
            pltpu.SemaphoreType.DMA((BOXES, 4)),
            pltpu.SemaphoreType.DMA((2,)),
        ],
        compiler_params=pltpu.CompilerParams(vmem_limit_bytes=VMEM_BYTES),
        cost_estimate=cost(1),
        name="skeletons",
    )(after, split, interp, cols, inverse, self_block)


def compact(payload, blocks, ids, sems):
    height = blocks.shape[0]
    return [
        pltpu.make_async_copy(payload.at[pl.ds(height, 8)], ids, sems.at[0]),
        pltpu.make_async_copy(payload.at[pl.ds(0, height)], blocks, sems.at[1]),
    ]


def merge_kernel(edge_h, payload, first_out, second_out, edge, blocks, ids, sems):
    copies = compact(payload, blocks, ids, sems) + [pltpu.make_async_copy(edge_h, edge, sems.at[2])]
    for copy in copies:
        copy.start()
    for copy in copies:
        copy.wait()

    def add(n, _):
        slot = ids[0, n].astype(jnp.int32)

        @pl.when(slot >= 0)
        def _():
            edge[slot] = edge[slot] + blocks[pl.ds(pl.multiple_of(n * SK, SK), SK), :]

        return 0

    lax.fori_loop(0, CAP, add, 0)
    outs = [
        pltpu.make_async_copy(edge.at[pl.ds(0, FIRST)], first_out, sems.at[0]),
        pltpu.make_async_copy(edge.at[pl.ds(FIRST, SLOTS - FIRST)], second_out, sems.at[1]),
    ]
    for copy in outs:
        copy.start()
    for copy in outs:
        copy.wait()


def merge(edge, payload):
    return pl.pallas_call(
        merge_kernel,
        out_shape=(block_type(FIRST), block_type(SLOTS - FIRST)),
        in_specs=[ANY, ANY],
        out_specs=(ANY, ANY),
        scratch_shapes=[
            pltpu.VMEM((SLOTS, SK, SK), F32),
            pltpu.VMEM((CAP * SK, SK), F32),
            pltpu.SMEM((8, 128), F32),
            pltpu.SemaphoreType.DMA((3,)),
        ],
        compiler_params=pltpu.CompilerParams(vmem_limit_bytes=VMEM_BYTES),
        cost_estimate=cost(1),
        name="merge",
    )(edge, payload)


def add_compact_kernel(total_h, payload, out, total, blocks, ids, sems):
    copies = compact(payload, blocks, ids, sems) + [pltpu.make_async_copy(total_h, total, sems.at[2])]
    for copy in copies:
        copy.start()
    for copy in copies:
        copy.wait()

    def add(n, _):
        slot = ids[0, n].astype(jnp.int32)

        @pl.when(slot >= 0)
        def _():
            total[slot] = total[slot] + blocks[pl.ds(pl.multiple_of(n * SK, SK), SK), :]

        return 0

    lax.fori_loop(0, CAP, add, 0)
    copy = pltpu.make_async_copy(total, out, sems.at[0])
    copy.start()
    copy.wait()


def add_compact(total, payload):
    return pl.pallas_call(
        add_compact_kernel,
        out_shape=block_type(SLOTS),
        in_specs=[ANY, ANY],
        out_specs=ANY,
        scratch_shapes=[
            pltpu.VMEM((SLOTS, SK, SK), F32),
            pltpu.VMEM((CAP * SK, SK), F32),
            pltpu.SMEM((8, 128), F32),
            pltpu.SemaphoreType.DMA((3,)),
        ],
        input_output_aliases={0: 0},
        compiler_params=pltpu.CompilerParams(vmem_limit_bytes=VMEM_BYTES),
        cost_estimate=cost(1000),
        name="add_compact",
    )(total, payload)


def add_dense_kernel(step, begin, total_h, arrived, out, total, blocks, sems):
    count = arrived.shape[0] // step
    loads = []
    for n in range(count):
        loads.append((
            pltpu.make_async_copy(total_h.at[pl.ds(begin + n * step, step)], total.at[n], sems.at[n, 0]),
            pltpu.make_async_copy(arrived.at[pl.ds(n * step, step)], blocks.at[n], sems.at[n, 1]),
        ))
    for pair in loads:
        for copy in pair:
            copy.start()
    stores = []
    for n in range(count):
        for copy in loads[n]:
            copy.wait()
        total[n] = total[n] + blocks[n]
        stores.append(pltpu.make_async_copy(total.at[n], out.at[pl.ds(begin + n * step, step)], sems.at[n, 2]))
        stores[n].start()
    for copy in stores:
        copy.wait()


def add_dense(total, arrived, begin, step):
    count = arrived.shape[0] // step
    return pl.pallas_call(
        functools.partial(add_dense_kernel, step, begin),
        out_shape=block_type(SLOTS),
        in_specs=[ANY, ANY],
        out_specs=ANY,
        scratch_shapes=[
            pltpu.VMEM((count, step, SK, SK), F32),
            pltpu.VMEM((count, step, SK, SK), F32),
            pltpu.SemaphoreType.DMA((count, 3)),
        ],
        input_output_aliases={0: 0},
        compiler_params=pltpu.CompilerParams(vmem_limit_bytes=VMEM_BYTES),
        cost_estimate=cost(1),
        name="add_dense",
    )(total, arrived)


def place_kernel(coarse, received, out, held, sems):
    parity = lax.rem(lax.axis_index("box"), 2)
    copy = pltpu.make_async_copy(received, held, sems.at[0])
    copy.start()
    copy.wait()
    copy = pltpu.make_async_copy(held, out.at[pl.ds(2 - 2 * parity, 2)], sems.at[1])
    copy.start()
    copy.wait()


def place(coarse, received):
    return pl.pallas_call(
        place_kernel,
        out_shape=jax.ShapeDtypeStruct(coarse.shape, F32),
        in_specs=[ANY, ANY],
        out_specs=ANY,
        scratch_shapes=[pltpu.VMEM((BOXES, NB // 2, SK, SK), F32), pltpu.SemaphoreType.DMA((2,))],
        input_output_aliases={0: 0},
        compiler_params=pltpu.CompilerParams(vmem_limit_bytes=VMEM_BYTES),
        cost_estimate=cost(1),
        name="place",
    )(coarse, received)


def moved(value, route):
    devices = lax.axis_size("box")
    return lax.ppermute(value, "box", [(i, route(i) % devices) for i in range(devices)])


def other_core(i):
    return i ^ 1


def across(i):
    return i + 1 if i % 2 else i - 1


def beyond(i):
    return i + 2 if i % 2 else i - 2


def body(self_block, interp, split, inverse_block, row_blocks, col_blocks, pairs, targets, pair_blocks):
    targets = jnp.transpose(targets, (0, 2, 1))
    pairs = jnp.transpose(pairs, (0, 2, 1))
    rows = row_blocks.reshape(BOXES, ROWS, P_SIZE)
    cols = col_blocks.reshape(BOXES, ROWS, P_SIZE)
    near, far = front(targets, pairs, split, interp, cols, rows, inverse_block)
    near = moved(near, beyond)
    far = moved(far, other_core)
    edge, partner, total = rest(targets, pairs, split, interp, cols, rows, inverse_block, pair_blocks)
    first, second = merge(edge, far)
    first = moved(first, across)
    second = moved(second, across)
    partner = moved(partner, other_core)
    total = add_compact(total, near)
    coarse, skel = skeletons(total, split, interp, cols, inverse_block, self_block)
    skel = moved(skel, other_core)
    coarse = place(coarse, skel)
    total = add_dense(total, partner, 0, 8)
    total = add_dense(total, second, FIRST, 4)
    total = add_dense(total, first, 0, 8)
    return total, coarse[None]


def solution(mesh):
    return jax.shard_map(
        body,
        mesh=mesh,
        in_specs=(
            P("box", None, None),
            P("box", None, None),
            P("box", None),
            P("box", None, None),
            P("box", None, None, None),
            P("box", None, None, None),
            P("box", None, None),
            P("box", None, None),
            P("box", None, None),
        ),
        out_specs=(P("box", None, None), P("box", None, None, None, None)),
        check_vma=False,
    )
```

time: 127 us -> 88.6 us (0.70); the launches traced: 125 us -> 88.7 us
  Pallas kernels: 74.8 us -> 55.6 us
  waiting for transfers between devices: 24 us -> 14.2 us
  starting transfers between devices: 21.8 us -> 17.1 us
  local copies, waits for them, and re-layouts: 4.05 us -> 0.8 us
    pallas_call x1, Pallas kernels: 17 us -> 1.85 us  [place(): pl.pallas_call(place_kernel, out_shape=jax.ShapeDtypeStruct(coarse.shape,...]
    ppermute x8 -> x6, waiting for transfers between devices: 24 us -> 14.2 us  [moved(): lax.ppermute(value, 'box', [(i, route(i) % devices) for i in range(device...]
    pallas_call x1, Pallas kernels: 20.6 us -> 15.3 us  [rest(): pl.pallas_call(rest_kernel, out_shape=(block_type(SLOTS), block_type(SLOT...]
    ppermute x8 -> x6, starting transfers between devices: 21.8 us -> 17.1 us  [moved(): lax.ppermute(value, 'box', [(i, route(i) % devices) for i in range(device...]
    unnamed x20 -> x2, local copies, waits for them, and re-layouts: 4.05 us -> 0.8 us
    pallas_call x3 -> x5, Pallas kernels: 27.6 us -> 28.8 us  [the longest x1 12.3 us: front(): pl.pallas_call(front_kernel, out_shape=(payload_type(CAP), payload_type(C...]
  transfers between devices with their start and end apart: 8 -> 6, of which waited for: 2 -> 2; matrix products, arithmetic and copies ran while one was open for 0% -> 0% of each run, Pallas kernels for 41% -> 45%
where the time goes in v1:
time: 88.6 us; the launch traced here: 88.7 us
  Pallas kernels  55.6 us (63%)
  starting transfers between devices  17.1 us (19%)
  waiting for transfers between devices  14.2 us (16%)
  between operations  0.9 us (1%)
    ppermute x6, starting transfers between devices, moved(): lax.ppermute(value, 'box', [(i, route(i) % devices) for i in range(device...  17.1 us
    pallas_call x1, Pallas kernels, rest(): pl.pallas_call(rest_kernel, out_shape=(block_type(SLOTS), block_type(SLOT...  15.3 us
    ppermute x6, waiting for transfers between devices, moved(): lax.ppermute(value, 'box', [(i, route(i) % devices) for i in range(device...  14.2 us
    pallas_call x1, Pallas kernels, front(): pl.pallas_call(front_kernel, out_shape=(payload_type(CAP), payload_type(C...  12.3 us
    pallas_call x3, Pallas kernels, add_dense(): pl.pallas_call(functools.partial(add_dense_kernel, step, begin), out_shap...  9.97 us
    pallas_call x1, Pallas kernels, skeletons(): pl.pallas_call(skeletons_kernel, out_shape=(jax.ShapeDtypeStruct((2 * BOX...  6.49 us
    pallas_call x1, Pallas kernels, add_compact(): pl.pallas_call(add_compact_kernel, out_shape=block_type(SLOTS), in_specs=...  4.85 us
    pallas_call x1, Pallas kernels, merge(): pl.pallas_call(merge_kernel, out_shape=(block_type(FIRST), block_type(SLO...  4.82 us
  transfers between devices with their start and end apart: 6, of which 2 were waited for; matrix products, arithmetic and copies ran while one was open for 0% of the time, Pallas kernels for 45%

profile of v1, /device:TPU:0, one launch (start us, length us, event | category | flops | bytes accessed | tf_op | source)
XLA Modules:
  0.0 88.7 jit_solution(3085932801553023158)
XLA Ops:
  0.6 12.3 %front.1 = (f32[4104,128]{1,0:T(8,128)}, f32[4104,128]{1,0:T(8,128)}) custom-call(s32[2,2,24]{2,1,0:T(2,128)} %bitcast.10, s32[2,2,24]{2,1,0:T(2,128)} %bitcast.12, s32[2,512]{1,0:T(2,128)} %split.5, bf16[2,384,128]{2,1,0:T(8,128)(2,1)} %interp_h.5, bf16[2,1024,512]{2,1,0:T(8,128)(2,1)} %bitcast.5, bf16[2,1024,512]{2,1,0:T(8,128)(2,1)} %bitcast.8, ...), custom_call_target="tpu_custom_call" | custom-call | flops 1000000000 | tf_op jit(solution)/shard_map/front/pallas_call | solution.py:216
  12.9 0.1 collective-permute-start.2
  13.0 9.6 %collective-permute-start = (f32[4104,128]{1,0:T(8,128)}, f32[4104,128]{1,0:T(8,128)}, u32[]{:S(2)}, u32[]{:S(2)}) collective-permute-start(f32[4104,128]{1,0:T(8,128)} %get-tuple-element.12), channel_id=1, source_target_pairs={{0,126},{1,3},{2,0},{3,5},{4,2},{5,7},{6,4},{7,9},{8,6},{9,11},{10... | collective-permute-start | bytes 6303752 | tf_op jit(solution)/shard_map/ppermute | solution.py:564
  22.7 15.3 %rest.1 = (f32[48,128,128]{2,1,0:T(8,128)}, f32[48,128,128]{2,1,0:T(8,128)}, f32[48,128,128]{2,1,0:T(8,128)}) custom-call(s32[2,2,24]{2,1,0:T(2,128)} %bitcast.11, s32[2,2,24]{2,1,0:T(2,128)} %bitcast.13, s32[2,512]{1,0:T(2,128)} %split.5, bf16[2,384,128]{2,1,0:T(8,128)(2,1)} %interp_h.5, bf16[2,1024,512]{2,1,0:T(8,128)(2,1)} %bitcast.6, ...), custom_call_target="tpu_custom_call" | custom-call | flops 1000000000 | tf_op jit(solution)/shard_map/rest/pallas_call | solution.py:325
  38.0 0.1 collective-permute-start.1
  38.1 0.0 collective-permute-done.2.payload
  38.1 4.8 %merge.1 = (f32[32,128,128]{2,1,0:T(8,128)}, f32[16,128,128]{2,1,0:T(8,128)}) custom-call(f32[48,128,128]{2,1,0:T(8,128)} %get-tuple-element.14.edge_h, f32[4104,128]{1,0:T(8,128)} %collective-permute-done.2.payload), custom_call_target="tpu_custom_call" | custom-call | flops 1000000000 | tf_op jit(solution)/shard_map/merge/pallas_call | solution.py:439
  42.9 0.2 collective-permute-start.3
  43.1 7.0 %collective-permute-start.4 = (f32[32,128,128]{2,1,0:T(8,128)}, f32[32,128,128]{2,1,0:T(8,128)}, u32[]{:S(2)}, u32[]{:S(2)}) collective-permute-start(f32[32,128,128]{2,1,0:T(8,128)} %get-tuple-element.17), channel_id=1, source_target_pairs={{0,127},{1,2},{2,1},{3,4},{4,3},{5,6},{6,5},{7,8},{8,7},{9,10},{10... | collective-permute-start | bytes 6291464 | tf_op jit(solution)/shard_map/ppermute | solution.py:564
  50.1 0.0 collective-permute-done.payload
  50.1 4.9 %add_compact.1.total_h.after = f32[48,128,128]{2,1,0:T(8,128)} custom-call(f32[48,128,128]{2,1,0:T(8,128)} %get-tuple-element.11.total_h, f32[4104,128]{1,0:T(8,128)} %collective-permute-done.payload), custom_call_target="tpu_custom_call", output_to_operand_aliasing={{}: (0, {})} | custom-call | flops 999999995904 | tf_op jit(solution)/shard_map/add_compact/pallas_call | solution.py:479
  55.0 6.5 %skeletons.1 = (f32[4,4,128,128]{3,2,1,0:T(8,128)}, f32[2,4,128,128]{3,2,1,0:T(8,128)}) custom-call(f32[48,128,128]{2,1,0:T(8,128)} %add_compact.1.total_h.after, s32[2,512]{1,0:T(2,128)} %split.5, bf16[2,384,128]{2,1,0:T(8,128)(2,1)} %interp_h.5, bf16[2,1024,512]{2,1,0:T(8,128)(2,1)} %bitcast.7, bf16[2,384,384]{2,1,0:T(8,128)(2,1)} %inverse_h.5, ...), custom_call_target="tpu_custom_call" | custom-call | flops 1000000000 | tf_op jit(solution)/shard_map/skeletons/pallas_call | solution.py:379
  61.5 0.1 collective-permute-start.5
  61.6 2.1 %collective-permute-done.5.received = f32[2,4,128,128]{3,2,1,0:T(8,128)S(1)} collective-permute-done((f32[2,4,128,128]{3,2,1,0:T(8,128)}, f32[2,4,128,128]{3,2,1,0:T(8,128)S(1)}, u32[]{:S(2)}, u32[]{:S(2)}) %collective-permute-start.5) | collective-permute-done | bytes 524320 | tf_op jit(solution)/shard_map/ppermute | solution.py:564
  63.7 0.0 copy-start
  63.7 0.8 copy-done
  64.5 1.8 %place.1 = f32[4,4,128,128]{3,2,1,0:T(8,128)} custom-call(f32[4,4,128,128]{3,2,1,0:T(8,128)} %get-tuple-element.18.coarse, f32[2,4,128,128]{3,2,1,0:T(8,128)} %copy-done), custom_call_target="tpu_custom_call", output_to_operand_aliasing={{}: (0, {})} | custom-call | flops 1000000000 | tf_op jit(solution)/shard_map/place/pallas_call | solution.py:549
  66.4 0.0 collective-permute-done.1.arrived
  66.4 4.5 %add_dense.3.total_h = f32[48,128,128]{2,1,0:T(8,128)} custom-call(f32[48,128,128]{2,1,0:T(8,128)} %add_compact.1.total_h.after, f32[48,128,128]{2,1,0:T(8,128)} %collective-permute-done.1.arrived), custom_call_target="tpu_custom_call", output_to_operand_aliasing={{}: (0, {})} | custom-call | flops 1000000000 | tf_op jit(solution)/shard_map/add_dense/pallas_call | solution.py:521
  70.9 0.0 collective-permute-done.3.arrived
  70.9 2.3 %add_dense.4.total_h = f32[48,128,128]{2,1,0:T(8,128)} custom-call(f32[48,128,128]{2,1,0:T(8,128)} %add_dense.3.total_h, f32[16,128,128]{2,1,0:T(8,128)} %collective-permute-done.3.arrived), custom_call_target="tpu_custom_call", output_to_operand_aliasing={{}: (0, {})} | custom-call | flops 1000000000 | tf_op jit(solution)/shard_map/add_dense/pallas_call | solution.py:521
  73.3 12.1 %collective-permute-done.4.arrived = f32[32,128,128]{2,1,0:T(8,128)} collective-permute-done((f32[32,128,128]{2,1,0:T(8,128)}, f32[32,128,128]{2,1,0:T(8,128)}, u32[]{:S(2)}, u32[]{:S(2)}) %collective-permute-start.4) | collective-permute-done | bytes 2097184 | tf_op jit(solution)/shard_map/ppermute | solution.py:564
  85.4 3.1 %add_dense.5 = f32[48,128,128]{2,1,0:T(8,128)} custom-call(f32[48,128,128]{2,1,0:T(8,128)} %add_dense.4.total_h, f32[32,128,128]{2,1,0:T(8,128)} %collective-permute-done.4.arrived), custom_call_target="tpu_custom_call", output_to_operand_aliasing={{}: (0, {})} | custom-call | flops 1000000000 | tf_op jit(solution)/shard_map/add_dense/pallas_call | solution.py:521
Async XLA Ops:
  12.9 25.1 %collective-permute-start.2 = (f32[4104,128]{1,0:T(8,128)}, f32[4104,128]{1,0:T(8,128)}, u32[]{:S(2)}, u32[]{:S(2)}) collective-permute-start(f32[4104,128]{1,0:T(8,128)} %get-tuple-element.15), channel_id=1, source_target_pairs={{0,1},{1,0},{2,3},{3,2},{4,5},{5,4},{6,7},{7,6},{8,9},{9,8},{10,11... | collective-permute-start | bytes 6303752 | tf_op jit(solution)/shard_map/ppermute | solution.py:564
  13.0 37.1 %collective-permute-start = (f32[4104,128]{1,0:T(8,128)}, f32[4104,128]{1,0:T(8,128)}, u32[]{:S(2)}, u32[]{:S(2)}) collective-permute-start(f32[4104,128]{1,0:T(8,128)} %get-tuple-element.12), channel_id=1, source_target_pairs={{0,126},{1,3},{2,0},{3,5},{4,2},{5,7},{6,4},{7,9},{8,6},{9,11},{10... | collective-permute-start | bytes 6303752 | tf_op jit(solution)/shard_map/ppermute | solution.py:564
  38.0 28.4 %collective-permute-start.1 = (f32[48,128,128]{2,1,0:T(8,128)}, f32[48,128,128]{2,1,0:T(8,128)}, u32[]{:S(2)}, u32[]{:S(2)}) collective-permute-start(f32[48,128,128]{2,1,0:T(8,128)} %get-tuple-element.13), channel_id=1, source_target_pairs={{0,1},{1,0},{2,3},{3,2},{4,5},{5,4},{6,7},{7,6},{8,9},{9,8},{10,11... | collective-permute-start | bytes 9437192 | tf_op jit(solution)/shard_map/ppermute | solution.py:564
  42.9 28.0 %collective-permute-start.3 = (f32[16,128,128]{2,1,0:T(8,128)}, f32[16,128,128]{2,1,0:T(8,128)}, u32[]{:S(2)}, u32[]{:S(2)}) collective-permute-start(f32[16,128,128]{2,1,0:T(8,128)} %get-tuple-element.16), channel_id=1, source_target_pairs={{0,127},{1,2},{2,1},{3,4},{4,3},{5,6},{6,5},{7,8},{8,7},{9,10},{10... | collective-permute-start | bytes 3145736 | tf_op jit(solution)/shard_map/ppermute | solution.py:564
  43.1 42.3 %collective-permute-start.4 = (f32[32,128,128]{2,1,0:T(8,128)}, f32[32,128,128]{2,1,0:T(8,128)}, u32[]{:S(2)}, u32[]{:S(2)}) collective-permute-start(f32[32,128,128]{2,1,0:T(8,128)} %get-tuple-element.17), channel_id=1, source_target_pairs={{0,127},{1,2},{2,1},{3,4},{4,3},{5,6},{6,5},{7,8},{8,7},{9,10},{10... | collective-permute-start | bytes 6291464 | tf_op jit(solution)/shard_map/ppermute | solution.py:564
  61.5 2.2 %collective-permute-start.5 = (f32[2,4,128,128]{3,2,1,0:T(8,128)}, f32[2,4,128,128]{3,2,1,0:T(8,128)S(1)}, u32[]{:S(2)}, u32[]{:S(2)}) collective-permute-start(f32[2,4,128,128]{3,2,1,0:T(8,128)} %get-tuple-element.19), channel_id=1, source_target_pairs={{0,1},{1,0},{2,3},{3,2},{4,5},{5,4},{6,7},{7,6},{8,9},{9,8},{10,11... | collective-permute-start | bytes 1572872 | tf_op jit(solution)/shard_map/ppermute | solution.py:564
  63.7 0.8 copy-start
